TPU v7x, 32 devices: a whole 2x2x4 slice. The times are simulated.
32 devices in a mesh: parts: 2 (over y), rows: 4 (over z), feat: 4 (over x, core).
Axes of the slice: x: 2, y: 2, z: 4, core: 2. Of those that a mesh axis runs over, the one named last changes fastest.
Arguments:
- tokens: bfloat16 [8192, 1024], P(('parts', 'rows')), parts along dimension 0
- cluster_id: int32 [8192, 1], P(('parts', 'rows')), parts along dimension 0, may hold values from 0 to 3; in each aligned block of 1024 rows (0 to 1023, 1024 to 2047, ...) at most 640 rows name the same one
- seeds: bfloat16 [8, 1024, 1024], P(('parts', 'rows'), 'feat'), parts along dimension 0
Outputs:
- centroids: bfloat16 [8, 1024, 1024], P(('parts', 'rows'), 'feat'), parts along dimension 0
- energy: float32 [8192], P(('parts', 'rows')), parts along dimension 0
There are 2 independent parts, one for each index of `parts`. A program takes and returns all parts, laid end to end along the dimension named above; each array names one. Nothing has to cross between parts.
Inputs may be any that keep to these rules, and one draw needn't show every extreme that they name: `cluster_id`: each aligned block of 1024 rows (the rows of one index of rows) names one cluster at most 640 times.
All inputs are finite; a program needn't handle non-finite values.
Results may differ from a plain program's by a relative error of at most 0.0059.
Values may be sent and summed in bfloat16 or wider, within the bound.
A program may use at most 64 MiB of HBM per device.

v0:
```python
import jax
import jax.numpy as jnp
from jax import lax
from jax.sharding import PartitionSpec as P

ITERS = 2


sharpness = 20.0
epsilon = 1e-06


def unit_rows(values):
    wide = values.astype(jnp.float32)
    return wide * lax.rsqrt(jnp.sum(wide * wide, axis=-1, keepdims=True) + epsilon)


def weights_of(members, current):
    cosine = jnp.dot(members, current.T, preferred_element_type=jnp.float32)
    weight = jnp.exp(sharpness * (cosine - 1.0))
    total = lax.psum(jnp.sum(weight, axis=1), "feat")
    return (weight, total)


def on_device(tokens, cluster_id, seeds):
    own_rows = tokens.shape[0]
    depth = tokens.shape[1]
    groups = lax.axis_size("rows")
    feats = lax.axis_size("feat")
    capacity = feats * ((5 * own_rows + 2 * groups * feats - 1) // (2 * groups * feats))
    unit = unit_rows(tokens).astype(jnp.bfloat16)
    labels = cluster_id[:, 0]
    onehot = (labels[:, None] == jnp.arange(groups, dtype=jnp.int32)[None, :]).astype(jnp.int32)
    earlier = jnp.cumsum(onehot, axis=0) - onehot
    placing = jnp.sum(earlier * onehot, axis=1)
    slot_of = labels * capacity + placing
    outgoing = jnp.zeros((groups * capacity, depth), jnp.bfloat16).at[slot_of].set(unit)
    outgoing = outgoing.reshape(groups, capacity, depth)
    arrived = lax.all_to_all(outgoing, "rows", split_axis=0, concat_axis=0, tiled=True)
    members = arrived.reshape(groups * capacity, depth)
    current = unit_rows(seeds[0]).astype(jnp.bfloat16)
    for step in range(ITERS):
        weight, total = weights_of(members, current)
        prob = (weight / total[:, None]).astype(jnp.bfloat16)
        moment = lax.dot_general(
            prob, members, (((0,), (0,)), ((), ())), preferred_element_type=jnp.float32
        )
        current = unit_rows(moment).astype(jnp.bfloat16)
    weight, total = weights_of(members, current)
    energies = (1.0 + jnp.log(total) / sharpness).reshape(groups, capacity)
    homeward = lax.all_to_all(energies, "rows", split_axis=0, concat_axis=0, tiled=True)
    energy = homeward.reshape(-1)[slot_of]
    return (current[None], energy)


def solution(mesh):
    in_specs = (
        P(("parts", "rows"), None),
        P(("parts", "rows"), None),
        P(("parts", "rows"), "feat", None),
    )
    out_specs = (P(("parts", "rows"), "feat", None), P(("parts", "rows")))
    return jax.shard_map(
        on_device, mesh=mesh, in_specs=in_specs, out_specs=out_specs, check_vma=False
    )
```

profile of v0, /device:TPU:0, one launch (start us, length us, event | category | flops | bytes accessed | tf_op | source)
XLA Modules:
  0.0 212.2 jit_solution(6814826184697484784)
XLA Ops:
  0.6 0.0 copy-start
  0.6 0.8 fusion.26
  1.5 1.1 reduce-window.6
  2.6 0.2 slice_reduce_fusion
  2.8 0.2 reduce-window.9
  3.0 0.1 add_bitcast_fusion
  3.1 0.7 fusion.25
  3.8 0.7 compare_select_fusion
  4.5 2.1 fusion
  6.6 0.0 copy-done
  6.6 8.9 %scatter_custom_fusion = bf16[2560,1024]{1,0:T(8,128)(2,1)} fusion(s32[1024]{0:T(1024)S(1)} %bitcast.40, bf16[]{:T(256)} %constant.10.clone.1, bf16[1024,1024]{1,0:T(8,128)(2,1)S(1)} %copy-done, f32[1024]{0:T(1024)S(1)} %add_rsqrt_fusion), kind=kCustom, calls=%fused_computation.17 | custom fusion | flops 3145728 | bytes 7344130 | tf_op jit(solution)/shard_map/scatter | solution.py:37
  15.5 0.0 copy-start.1
  15.5 6.4 %all-to-all-start = ((bf16[4,640,1024]{2,1,0:T(8,128)(2,1)}), bf16[4,640,1024]{2,1,0:T(8,128)(2,1)}, u32[]{:S(2)}, u32[]{:S(2)}) async-start(bf16[4,640,1024]{2,1,0:T(8,128)(2,1)} %bitcast.37), calls=%async_computation | async-start | bytes 10485760 | tf_op jit(solution)/shard_map/all_to_all | solution.py:39
  22.0 0.0 copy-done.1
  22.0 0.2 fusion.17
  22.2 115.9 %all-to-all-done = bf16[4,640,1024]{2,1,0:T(8,128)(2,1)} async-done(((bf16[4,640,1024]{2,1,0:T(8,128)(2,1)}), bf16[4,640,1024]{2,1,0:T(8,128)(2,1)}, u32[]{:S(2)}, u32[]{:S(2)}) %all-to-all-start) | async-done | bytes 5242912 | tf_op jit(solution)/shard_map/all_to_all | solution.py:39
  138.1 4.3 %fusion.28 = (f32[2560]{0:T(1024)S(1)}, f32[2560,256]{0,1:T(8,128)S(1)}) fusion(bf16[2560,1024]{1,0:T(8,128)(2,1)} %bitcast.6, bf16[1,256,1024]{2,1,0:T(8,128)(2,1)S(1)} %copy-done.1, f32[256]{0:T(256)S(1)} %add_rsqrt_fusion.3), kind=kOutput, calls=%fused_computation.53 | convolution fusion | flops 1344927232 | bytes 8399872 | tf_op jit(solution)/shard_map/dot_general | solution.py:19
  142.5 10.1 %psum.21 = f32[2560]{0:T(1024)S(1)} all-reduce(f32[2560]{0:T(1024)S(1)} %get-tuple-element.2), channel_id=1, replica_groups=mesh['parts'=2,'rows'=4,'feat'=4] {'feat'}, use_global_device_ids=true, to_apply=%region_7.8 | all-reduce | flops 2560 | bytes 20480 | tf_op jit(solution)/shard_map/psum | solution.py:21
  152.6 4.2 %multiply_reduce_fusion.1 = (f32[256]{0:T(256)S(1)}, f32[256,1024]{1,0:T(8,128)S(1)}) fusion(bf16[2560,1024]{1,0:T(8,128)(2,1)} %bitcast.6, f32[2560,256]{0,1:T(8,128)S(1)} %get-tuple-element.3, f32[2560]{0:T(1024)S(1)} %psum.21), kind=kOutput, calls=%fused_computation.32 | convolution fusion | flops 1344012032 | bytes 8924160 | tf_op jit(solution)/shard_map/dot_general | solution.py:45
  156.8 5.8 %fusion.29 = (f32[2560]{0:T(1024)S(1)}, f32[2560,256]{0,1:T(8,128)}) fusion(bf16[2560,1024]{1,0:T(8,128)(2,1)} %bitcast.6, f32[256,1024]{1,0:T(8,128)S(1)} %get-tuple-element.5, f32[256]{0:T(256)S(1)} %add_rsqrt_fusion.2), kind=kOutput, calls=%fused_computation.54 | convolution fusion | flops 1344665088 | bytes 8924160 | tf_op jit(solution)/shard_map/dot_general | solution.py:19
  162.6 10.3 %psum.22 = f32[2560]{0:T(1024)S(1)} all-reduce(f32[2560]{0:T(1024)S(1)} %get-tuple-element.6), channel_id=1, replica_groups=mesh['parts'=2,'rows'=4,'feat'=4] {'feat'}, use_global_device_ids=true, to_apply=%region_10.11 | all-reduce | flops 2560 | bytes 20480 | tf_op jit(solution)/shard_map/psum | solution.py:21
  172.9 4.9 %multiply_reduce_fusion = (f32[256]{0:T(256)S(1)}, f32[256,1024]{1,0:T(8,128)S(1)}) fusion(bf16[2560,1024]{1,0:T(8,128)(2,1)} %bitcast.6, f32[2560,256]{0,1:T(8,128)} %get-tuple-element.7, f32[2560]{0:T(1024)S(1)} %psum.22), kind=kOutput, calls=%fused_computation.30 | convolution fusion | flops 1344012032 | bytes 8924160 | tf_op jit(solution)/shard_map/dot_general | solution.py:45
  177.8 4.3 %fusion.12 = f32[2560]{0:T(1024)S(1)} fusion(bf16[2560,1024]{1,0:T(8,128)(2,1)} %bitcast.6, f32[256,1024]{1,0:T(8,128)S(1)} %get-tuple-element.9, f32[256]{0:T(256)S(1)} %add_rsqrt_fusion.1), kind=kOutput, calls=%fused_computation.20 | convolution fusion | flops 1344665088 | bytes 6302720 | tf_op jit(solution)/shard_map/dot_general | solution.py:19
  182.1 10.1 %psum.23 = f32[2560]{0:T(1024)S(1)} all-reduce(f32[2560]{0:T(1024)S(1)} %fusion.12), channel_id=1, replica_groups=mesh['parts'=2,'rows'=4,'feat'=4] {'feat'}, use_global_device_ids=true, to_apply=%region_13.14 | all-reduce | flops 2560 | bytes 20480 | tf_op jit(solution)/shard_map/psum | solution.py:21
  192.2 0.6 all_to_all.10
  192.8 3.2 %all-to-all-start.1 = ((f32[4,1,640]{2,1,0:T(1,128)}), f32[4,1,640]{2,1,0:T(1,128)S(1)}, u32[]{:S(2)}, u32[]{:S(2)}) async-start(f32[4,1,640]{2,1,0:T(1,128)} %all_to_all.10), calls=%async_computation.1 | async-start | bytes 20480 | tf_op jit(solution)/shard_map/all_to_all | solution.py:51
  196.1 0.9 fusion.27
  197.0 4.6 %all-to-all-done.1 = f32[4,1,640]{2,1,0:T(1,128)S(1)} async-done(((f32[4,1,640]{2,1,0:T(1,128)}), f32[4,1,640]{2,1,0:T(1,128)S(1)}, u32[]{:S(2)}, u32[]{:S(2)}) %all-to-all-start.1) | async-done | bytes 10272 | tf_op jit(solution)/shard_map/all_to_all | solution.py:51
  201.7 10.5 %gather_fusion = f32[1024]{0:T(1024)} fusion(f32[2560]{0:T(1024)S(1)} %reshape.74, s32[1024]{0:T(1024)S(1)} %broadcast_clamp_fusion), kind=kCustom, calls=%fused_computation | custom fusion | bytes 12288 | tf_op jit(solution)/shard_map/gather | solution.py:52
  (8 shorter events, 0.1 us)
Async XLA Ops:
  0.6 6.0 %copy-start = (bf16[1024,1024]{1,0:T(8,128)(2,1)S(1)}, bf16[1024,1024]{1,0:T(8,128)(2,1)}, u32[]{:S(2)}) copy-start(bf16[1024,1024]{1,0:T(8,128)(2,1)} %param.3) | copy-start | bytes 6291460
  15.5 6.5 %copy-start.1 = (bf16[1,256,1024]{2,1,0:T(8,128)(2,1)S(1)}, bf16[1,256,1024]{2,1,0:T(8,128)(2,1)}, u32[]{:S(2)}) copy-start(bf16[1,256,1024]{2,1,0:T(8,128)(2,1)} %param.5) | copy-start | bytes 1572868
  15.5 122.6 %all-to-all-start = ((bf16[4,640,1024]{2,1,0:T(8,128)(2,1)}), bf16[4,640,1024]{2,1,0:T(8,128)(2,1)}, u32[]{:S(2)}, u32[]{:S(2)}) async-start(bf16[4,640,1024]{2,1,0:T(8,128)(2,1)} %bitcast.37), calls=%async_computation | async-start | bytes 10485760 | tf_op jit(solution)/shard_map/all_to_all | solution.py:39
  192.8 8.8 %all-to-all-start.1 = ((f32[4,1,640]{2,1,0:T(1,128)}), f32[4,1,640]{2,1,0:T(1,128)S(1)}, u32[]{:S(2)}, u32[]{:S(2)}) async-start(f32[4,1,640]{2,1,0:T(1,128)} %all_to_all.10), calls=%async_computation.1 | async-start | bytes 20480 | tf_op jit(solution)/shard_map/all_to_all | solution.py:51
where the time goes:
time: 213 us; the launch traced here: 212 us
  waiting for transfers between devices  121 us (57%)
  blocking collectives  30.5 us (14%)
  matrix products  23.5 us (11%)
  other arithmetic  15.8 us (7%)
  local copies, waits for them, and re-layouts  11.4 us (5%)
  starting transfers between devices  9.7 us (5%)
    all_to_all x1, waiting for transfers between devices, on_device(): lax.all_to_all(outgoing, 'rows', split_axis=0, concat_axis=0, tiled=True)  116 us
    psum x3, blocking collectives, weights_of(): total = lax.psum(jnp.sum(weight, axis=1), 'feat')  30.5 us
    dot_general x3, matrix products, weights_of(): cosine = jnp.dot(members, current.T, preferred_element_type=jnp.float32)  14.5 us
    gather x1, local copies, waits for them, and re-layouts, on_device(): energy = homeward.reshape(-1)[slot_of]  10.5 us
    dot_general x2, matrix products, on_device(): lax.dot_general(prob, members, (((0,), (0,)), ((), ())), preferred_elemen...  9.05 us
    scatter x1, other arithmetic, on_device(): jnp.zeros((groups * capacity, depth), jnp.bfloat16).at[slot_of].set(unit)  8.95 us
    all_to_all x1, starting transfers between devices, on_device(): lax.all_to_all(outgoing, 'rows', split_axis=0, concat_axis=0, tiled=True)  6.45 us
    all_to_all x1, waiting for transfers between devices, on_device(): lax.all_to_all(energies, 'rows', split_axis=0, concat_axis=0, tiled=True)  4.64 us
  transfers between devices with their start and end apart: 2, of which 2 were waited for; matrix products, arithmetic and copies ran while one was open for 1% of the time, Pallas kernels for 0%

commit v1 on v0

v1 whole, which is shorter than its diff:
```python
import functools

import jax
import jax.numpy as jnp
from jax import lax
from jax.experimental import pallas as pl
from jax.experimental.pallas import tpu as pltpu
from jax.sharding import PartitionSpec as P

ITERS = 2
LANES = 128
SUBLANES = 8
SHARPNESS = 20.0
EPSILON = 1e-06
MESH = pl.DeviceIdType.MESH
F32 = jnp.float32
BF16 = jnp.bfloat16


def unit_rows(wide):
    return wide * lax.rsqrt(jnp.sum(wide * wide, axis=-1, keepdims=True) + EPSILON)


def steps(low, high, body):
    if high - low <= 8:
        for k in range(low, high):
            body(k)
    else:
        pl.loop(low, high)(body)


def when(condition, body):
    if isinstance(condition, bool):
        if condition:
            body()
    else:
        pl.when(condition)(body)


def kernel(groups, feats, chunk, parts_of_chunk, tokens_ref, label_ref, seeds_ref, cent_ref, energy_ref,
           members, outgoing, current, weight, moment, totals, ending, endings,
           zsend, xsend, csend, fsend, arrive, tsend, trecv, esend, erecv):
    me = lax.axis_index("rows")
    ft = lax.axis_index("feat")
    far = lax.rem(ft + 2, feats)
    sib = ft + 1 - 2 * lax.rem(ft, 2)
    farsib = lax.rem(sib + 2, feats)
    own_rows = tokens_ref.shape[0]
    slots = feats * chunk
    sub = chunk // parts_of_chunk
    ranks8 = totals.shape[-2]
    nsplit = slots // LANES

    barrier = pltpu.get_barrier_semaphore()

    def greet(k):
        for j in range(feats):
            if isinstance(k, int) and k == 0 and j == 0:
                continue
            pl.semaphore_signal(
                barrier, inc=1,
                device_id={"rows": lax.rem(me + k, groups), "feat": lax.rem(ft + j, feats)},
                device_id_type=MESH)

    greet(0)
    steps(1, groups, greet)

    tri = (lax.broadcasted_iota(jnp.int32, (LANES, LANES), 0)
           < lax.broadcasted_iota(jnp.int32, (LANES, LANES), 1)).astype(BF16)
    high = max(SUBLANES, groups)
    carry = jnp.zeros((high, 1), F32)
    ranks = []
    for b in range(own_rows // LANES):
        lab = label_ref[:, b * LANES:(b + 1) * LANES]
        hit = lax.broadcasted_iota(jnp.int32, (high, LANES), 0) == lab
        hot = jnp.where(hit, 1.0, 0.0)
        before = jnp.dot(hot.astype(BF16), tri, preferred_element_type=F32) + carry
        ranks.append(jnp.sum(hot * before, axis=0, keepdims=True))
        carry = carry + jnp.sum(hot, axis=1, keepdims=True)
    rank = jnp.concatenate(ranks, axis=1).astype(jnp.int32)
    label = label_ref[...]
    slot = label * slots + rank

    def picked(base, count):
        hot = (lax.broadcasted_iota(jnp.int32, (count, own_rows), 0) + base == slot)
        rows = jnp.dot(jnp.where(hot, 1.0, 0.0).astype(BF16), tokens_ref[...], preferred_element_type=F32)
        return unit_rows(rows).astype(BF16)

    def span(quarter, h):
        return pl.ds(pl.multiple_of(quarter * chunk + h * sub, 16), sub)

    def zcopy(k, h, dest, source):
        return pltpu.make_async_remote_copy(
            src_ref=outgoing.at[k, pl.ds(h * sub, sub)], dst_ref=members.at[source, span(ft, h)],
            send_sem=zsend.at[k, h], recv_sem=arrive.at[source, ft, h],
            device_id={"rows": dest}, device_id_type=MESH)

    def fcopy(source, quarter, h, peer, sem):
        place = members.at[source, span(quarter, h)]
        return pltpu.make_async_remote_copy(
            src_ref=place, dst_ref=place, send_sem=sem.at[source, h], recv_sem=arrive.at[source, quarter, h],
            device_id={"feat": peer}, device_id_type=MESH)

    def send_out(k):
        dest = lax.rem(me + k, groups)
        outgoing[k] = picked(dest * slots + ft * chunk, chunk)
        if isinstance(k, int) and k == 1:
            pl.semaphore_wait(barrier, groups * feats - 1)
        for h in range(parts_of_chunk):
            zcopy(k, h, dest, me).start()

    send_out(1)
    steps(2, groups, send_out)
    members[me] = picked(me * slots, slots)
    current[...] = unit_rows(seeds_ref[...].astype(F32)).astype(BF16)

    def weigh(s):
        cosine = lax.dot_general(current[...], members[s], (((1,), (1,)), ((), ())), preferred_element_type=F32)
        return jnp.exp(SHARPNESS * (cosine - 1.0))

    def folded(w):
        t = jnp.sum(w, axis=0, keepdims=True)
        rows = [t[:, j * LANES:(j + 1) * LANES] for j in range(nsplit)]
        rows.append(jnp.ones((ranks8 - nsplit, LANES), F32))
        return jnp.concatenate(rows, axis=0)

    def tcopy(it, s, owner, j, peer):
        place = totals.at[it, owner, s]
        return pltpu.make_async_remote_copy(
            src_ref=place, dst_ref=place, send_sem=tsend.at[it, s, j], recv_sem=trecv.at[it, s, owner],
            device_id={"feat": peer}, device_id_type=MESH)

    peers = [lax.rem(ft + j, feats) for j in range(feats)]

    def cos_block(it, s):
        w = weigh(s)
        weight[s] = w
        totals[it, ft, s] = folded(w)
        for j in range(1, feats):
            tcopy(it, s, ft, j, peers[j]).start()

    def prob_block(it, s):
        for j in range(1, feats):
            tcopy(it, s, peers[j], j, peers[j]).wait_recv()
        total = totals[it, 0, s]
        for j in range(1, feats):
            total = total + totals[it, j, s]
        inverse = 1.0 / total
        cut = [(weight[s, :, j * LANES:(j + 1) * LANES] * inverse[j:j + 1, :]).astype(BF16) for j in range(nsplit)]
        return jnp.concatenate(cut, axis=1)

    def add_block(it, s):
        moment[...] += jnp.dot(prob_block(it, s), members[s], preferred_element_type=F32)

    moment[...] = jnp.zeros_like(moment)

    def source_of(k):
        return lax.rem(me - k + groups, groups)

    cos_block(0, me)

    def overlapped(k):
        def landed():
            s = source_of(k)
            for h in range(parts_of_chunk):
                zcopy(0, h, s, s).wait_recv()
                fcopy(s, ft, h, far, xsend).start()
                fcopy(s, ft, h, sib, csend).start()

        def crossed():
            s = source_of(k - 1)
            for h in range(parts_of_chunk):
                fcopy(s, far, h, far, xsend).wait_recv()
                fcopy(s, far, h, sib, fsend).start()

        def whole():
            s = source_of(k - 1)
            for h in range(parts_of_chunk):
                fcopy(s, sib, h, sib, csend).wait_recv()
                fcopy(s, farsib, h, sib, fsend).wait_recv()
            cos_block(0, s)

        when(k < groups, landed)
        when(k >= 2, crossed)
        when(k >= 2, whole)
        when(k >= 2, lambda: add_block(0, source_of(k - 2)))

    steps(1, groups + 1, overlapped)
    add_block(0, source_of(groups - 1))
    current[...] = unit_rows(moment[...]).astype(BF16)

    for it in range(1, ITERS):
        steps(0, groups, lambda k: cos_block(it, source_of(k)))
        moment[...] = jnp.zeros_like(moment)
        steps(0, groups, lambda k: add_block(it, source_of(k)))
        current[...] = unit_rows(moment[...]).astype(BF16)

    cent_ref[...] = current[...]

    def ecopy(k, j, sender_row, sender_feat, s, peer):
        return pltpu.make_async_remote_copy(
            src_ref=ending.at[s], dst_ref=endings.at[sender_feat, sender_row],
            send_sem=esend.at[k, j], recv_sem=erecv.at[sender_feat, sender_row],
            device_id={"rows": s, "feat": peer}, device_id_type=MESH)

    def end_block(k):
        s = source_of(k)
        value = folded(weigh(s))
        ending[s] = value
        first = 0
        if isinstance(k, int) and k == 0:
            endings[ft, me] = value
            first = 1
        for j in range(first, feats):
            ecopy(k, j, me, ft, s, peers[j]).start()

    steps(1, groups, end_block)
    end_block(0)

    def end_wait(k):
        s = source_of(k)
        for j in range(1 if isinstance(k, int) and k == 0 else 0, feats):
            ecopy(k, j, s, peers[j], s, peers[j]).wait_recv()

    steps(1, groups, end_wait)
    end_wait(0)
    total = endings[0]
    for j in range(1, feats):
        total = total + endings[j]
    energy = (1.0 + jnp.log(total) / SHARPNESS).reshape(groups * ranks8, LANES)
    lead = energy.astype(BF16)
    rest = energy - lead.astype(F32)
    mid = rest.astype(BF16)
    low = (rest - mid.astype(F32)).astype(BF16)
    lane = jnp.where(lax.broadcasted_iota(jnp.int32, (LANES, own_rows), 0) == lax.rem(rank, LANES), 1.0, 0.0).astype(BF16)
    taken = (jnp.dot(lead, lane, preferred_element_type=F32)
             + jnp.dot(mid, lane, preferred_element_type=F32)
             + jnp.dot(low, lane, preferred_element_type=F32))
    line = lax.broadcasted_iota(jnp.int32, (groups * ranks8, own_rows), 0) == label * ranks8 + lax.div(rank, LANES)
    energy_ref[...] = jnp.sum(jnp.where(line, taken, 0.0), axis=0, keepdims=True)

    def drain(k):
        s = source_of(k)
        for h in range(parts_of_chunk):
            zcopy(k, h, s, me).wait_send()
            fcopy(s, ft, h, far, xsend).wait_send()
            fcopy(s, ft, h, sib, csend).wait_send()
            fcopy(s, far, h, sib, fsend).wait_send()

    def drain_small(k):
        s = source_of(k)
        for it in range(ITERS):
            for j in range(1, feats):
                tcopy(it, s, ft, j, peers[j]).wait_send()
        for j in range(1 if isinstance(k, int) and k == 0 else 0, feats):
            ecopy(k, j, me, ft, s, peers[j]).wait_send()

    steps(1, groups, drain)
    steps(1, groups, drain_small)
    drain_small(0)


def on_device(tokens, cluster_id, seeds):
    own_rows, depth = tokens.shape
    groups = lax.axis_size("rows")
    feats = lax.axis_size("feat")
    fine = seeds.shape[1]
    capacity = (5 * own_rows + 2 * groups - 1) // (2 * groups)
    chunk = -(-capacity // (feats * 32)) * 32
    pieces = 2
    slots = feats * chunk
    ranks8 = -(-(slots // LANES + 1) // SUBLANES) * SUBLANES
    sem = pltpu.SemaphoreType.DMA
    vmem = pl.BlockSpec(memory_space=pltpu.VMEM)
    centroids, energy = pl.pallas_call(
        functools.partial(kernel, groups, feats, chunk, pieces),
        out_shape=(jax.ShapeDtypeStruct((fine, depth), BF16), jax.ShapeDtypeStruct((1, own_rows), F32)),
        in_specs=[vmem, vmem, vmem],
        out_specs=(vmem, vmem),
        scratch_shapes=[
            pltpu.VMEM((groups, slots, depth), BF16),
            pltpu.VMEM((groups, chunk, depth), BF16),
            pltpu.VMEM((fine, depth), BF16),
            pltpu.VMEM((groups, fine, slots), F32),
            pltpu.VMEM((fine, depth), F32),
            pltpu.VMEM((ITERS, feats, groups, ranks8, LANES), F32),
            pltpu.VMEM((groups, ranks8, LANES), F32),
            pltpu.VMEM((feats, groups, ranks8, LANES), F32),
            sem((groups, pieces)), sem((groups, pieces)), sem((groups, pieces)), sem((groups, pieces)),
            sem((groups, feats, pieces)),
            sem((ITERS, groups, feats)), sem((ITERS, groups, feats)),
            sem((groups, feats)), sem((feats, groups)),
        ],
        compiler_params=pltpu.CompilerParams(
            collective_id=0, has_side_effects=True, vmem_limit_bytes=56 * 1024 * 1024),
    )(tokens, cluster_id.reshape(1, own_rows), seeds[0])
    return centroids[None], energy.reshape(own_rows)


def solution(mesh):
    in_specs = (
        P(("parts", "rows"), None),
        P(("parts", "rows"), None),
        P(("parts", "rows"), "feat", None),
    )
    out_specs = (P(("parts", "rows"), "feat", None), P(("parts", "rows")))
    return jax.shard_map(
        on_device, mesh=mesh, in_specs=in_specs, out_specs=out_specs, check_vma=False
    )
```

time: 213 us -> 72.7 us (0.34)
  waiting for transfers between devices: 121 us -> 0 us
  Pallas kernels: 0 us -> 68.7 us
  blocking collectives: 30.5 us -> 0 us
  matrix products: 23.5 us -> 0 us
  other arithmetic: 15.8 us -> 0 us
  starting transfers between devices: 9.7 us -> 0 us
  local copies, waits for them, and re-layouts: 11.4 us -> 3.13 us
    all_to_all x2 -> x0, waiting for transfers between devices: 121 us -> none  [the longest x1 116 us: on_device(): lax.all_to_all(outgoing, 'rows', split_axis=0, concat_axis=0, tiled=True)]
    pallas_call x0 -> x1, Pallas kernels: none -> 68.7 us  [on_device(): pl.pallas_call(functools.partial(kernel, groups, feats, chunk, pieces), o...]
    psum x3 -> x0, blocking collectives: 30.5 us -> none  [weights_of(): total = lax.psum(jnp.sum(weight, axis=1), 'feat')]
    dot_general x5 -> x0, matrix products: 23.5 us -> none  [the longest x3 14.5 us: weights_of(): cosine = jnp.dot(members, current.T, preferred_element_type=jnp.float32)]
    gather x1 -> x0, local copies, waits for them, and re-layouts: 10.5 us -> none  [on_device(): energy = homeward.reshape(-1)[slot_of]]
    all_to_all x2 -> x0, starting transfers between devices: 9.7 us -> none  [the longest x1 6.45 us: on_device(): lax.all_to_all(outgoing, 'rows', split_axis=0, concat_axis=0, tiled=True)]
    scatter x1 -> x0, other arithmetic: 8.95 us -> none  [on_device(): jnp.zeros((groups * capacity, depth), jnp.bfloat16).at[slot_of].set(unit)]
    unnamed x4 -> x2, local copies, waits for them, and re-layouts: 0.01 us -> 3.13 us
  transfers between devices with their start and end apart: 2 -> 0, of which waited for: 2 -> 0; matrix products, arithmetic and copies ran while one was open for 1% -> 0% of each run, Pallas kernels for 0% -> 0%
where the time goes in v1:
time: 72.7 us; the launch traced here: 72.5 us
  Pallas kernels  68.7 us (94%)
  local copies, waits for them, and re-layouts  3.13 us (4%)
    pallas_call x1, Pallas kernels, on_device(): pl.pallas_call(functools.partial(kernel, groups, feats, chunk, pieces), o...  68.7 us
    unnamed x2, local copies, waits for them, and re-layouts  3.13 us

profile of v1, /device:TPU:0, one launch (start us, length us, event | category | flops | bytes accessed | tf_op | source)
XLA Modules:
  0.0 72.5 jit_solution(16682385351276984325)
XLA Ops:
  0.6 68.7 %shard_map.50 = (bf16[256,1024]{1,0:T(8,128)(2,1)}, f32[1,1024]{1,0:T(1,128)}) custom-call(bf16[1024,1024]{1,0:T(8,128)(2,1)} %tokens_ref.1, s32[1,1024]{1,0:T(1,128)} %bitcast.6, bf16[256,1024]{1,0:T(8,128)(2,1)} %bitcast.4), custom_call_target="tpu_custom_call" | custom-call | tf_op jit(solution)/shard_map/pallas_call | solution.py:275
  69.4 1.9 %copy.7 = bf16[1,256,1024]{2,1,0:T(8,128)(2,1)} copy(bf16[1,256,1024]{2,1,0:T(8,128)(2,1)} %bitcast.5) | data formatting | bytes 1048576
  71.2 1.3 %copy.8 = f32[1024]{0:T(1024)} copy(f32[1024]{0:T(1024)} %bitcast.7) | data formatting | bytes 8192
